TPU v7x, 512 devices: a whole 4x8x8 slice. The times are simulated.
512 devices in a mesh: blk: 128 (over y, x_lo, z), grp: 4 (over x_hi, core).
Axes of the slice: x: 4 (x_hi: 2, x_lo: 2; x = x_hi * 2 + x_lo), y: 8, z: 8, core: 2. Of those that a mesh axis runs over, the one named last changes fastest.
Arguments:
- camera_vectors: bfloat16 [98304, 768], P(('blk', 'grp')), may hold values from -2 to 2
- command_vectors: bfloat16 [98304, 768], P(('blk', 'grp')), may hold values from -2 to 2
- sharpness_array: float32 [1], replicated, may hold values from 4 to 12
- offset_shift_array: float32 [1], replicated, may hold values from -3 to -1
Outputs:
- grad_frames: float32 [98304, 768], P(('blk', 'grp'))
- grad_instructions: float32 [98304, 768], P(('blk', 'grp'))
All inputs are finite; a program needn't handle non-finite values.
Results may differ from a plain program's by a relative error of at most 0.014.
Values may be sent and summed in bfloat16 or wider, within the bound.
A program may use at most 64 MiB of HBM per device.

v0:
```python
import jax
import jax.numpy as jnp
from jax import lax
from jax.sharding import PartitionSpec as P

STEPS = 6


def passed_along(value, axis, steps):
    count = lax.axis_size(axis)
    pairs = [(source, (source + steps) % count) for source in range(count)]
    return lax.ppermute(value, axis, pairs)


def unit_rows(values):
    wide = values.astype(jnp.float32)
    scale = lax.rsqrt(jnp.sum(wide * wide, axis=-1, keepdims=True) + 1e-06)
    return (wide * scale, scale)


def back_rows(unit, scale, grad):
    return scale * (grad - unit * jnp.sum(unit * grad, axis=-1, keepdims=True))


def fetch_direct(source, offset):
    return passed_along(source, "blk", -offset)


def local(camera_vectors, command_vectors, sharpness_array, offset_shift_array):
    rows = camera_vectors.shape[0]
    groups = lax.axis_size("grp")
    member = lax.axis_index("grp")
    unit_x, inv_x = unit_rows(camera_vectors)
    unit_y, inv_y = unit_rows(command_vectors)
    xb = unit_x.astype(jnp.bfloat16)
    yb = unit_y.astype(jnp.bfloat16)
    score_multiplier = sharpness_array[0]
    logit_bias = offset_shift_array[0]
    lowest = -(STEPS // 2)
    highest = lowest + STEPS - 1
    source = lax.all_gather(yb, "grp", axis=0, tiled=True)
    fetched = {0: source}
    for offset in range(lowest, highest + 1):
        if offset != 0:
            fetched[offset] = fetch_direct(source, offset)
    block = rows * groups
    columns = lax.broadcasted_iota(jnp.int32, (rows, block), 1)
    row_ids = lax.broadcasted_iota(jnp.int32, (rows, block), 0)
    matched_pairs = columns == member * rows + row_ids
    grad_x = jnp.zeros((rows, camera_vectors.shape[1]), jnp.float32)
    returned = jnp.zeros((block, camera_vectors.shape[1]), jnp.float32)
    for offset in range(lowest, highest + 1):
        yblock = fetched[offset]
        logits = (
            score_multiplier
            * lax.dot_general(
                xb, yblock, (((1,), (1,)), ((), ())), preferred_element_type=jnp.float32
            )
            + logit_bias
        )
        if offset == 0:
            label = jnp.where(matched_pairs, 1.0, -1.0).astype(jnp.float32)
        else:
            label = -jnp.ones_like(logits)
        coef = (-label * score_multiplier * jax.nn.sigmoid(-label * logits)).astype(jnp.bfloat16)
        grad_x = grad_x + jnp.dot(coef, yblock, preferred_element_type=jnp.float32)
        partial_value = lax.dot_general(
            coef, xb, (((0,), (0,)), ((), ())), preferred_element_type=jnp.float32
        ).astype(jnp.bfloat16)
        if offset == 0:
            returned = returned + partial_value.astype(jnp.float32)
        else:
            returned = returned + passed_along(partial_value, "blk", offset).astype(jnp.float32)
    grad_y = lax.psum_scatter(
        returned.astype(jnp.bfloat16), "grp", scatter_dimension=0, tiled=True
    ).astype(jnp.float32)
    return (back_rows(unit_x, inv_x, grad_x), back_rows(unit_y, inv_y, grad_y))


def solution(mesh):
    in_specs = (P(("blk", "grp"), None), P(("blk", "grp"), None), P(), P())
    out_specs = (P(("blk", "grp"), None), P(("blk", "grp"), None))
    return jax.shard_map(local, mesh=mesh, in_specs=in_specs, out_specs=out_specs, check_vma=False)
```

profile of v0, /device:TPU:1, one launch (start us, length us, event | category | flops | bytes accessed | tf_op | source)
XLA Modules:
  0.0 437.0 jit_solution(15256968533887606551)
XLA Ops:
  7.2 0.0 copy-start
  7.2 0.0 all-gather.2.cloned.1.call-start
  7.2 1.1 fusion.55
  8.4 1.8 fusion.47
  10.2 0.0 all-gather.2.cloned.1.call-update
  10.2 0.0 reduce-scatter.2.cloned.1.call-start
  10.2 33.2 %all-gather.2.cloned.1.call-done = bf16[768,768]{1,0:T(8,128)(2,1)} async-done(((bf16[192,768]{1,0:T(8,128)(2,1)}), bf16[768,768]{1,0:T(8,128)(2,1)}) %all-gather.2.cloned.1.call-update) | async-done | bytes 1179664 | tf_op jit(solution)/shard_map/all_gather | solution.py:41
  43.4 8.6 %collective-permute-start.4 = (bf16[768,768]{1,0:T(8,128)(2,1)}, bf16[768,768]{1,0:T(8,128)(2,1)S(1)}, u32[]{:S(2)}, u32[]{:S(2)}) collective-permute-start(bf16[768,768]{1,0:T(8,128)(2,1)} %all-gather.2.cloned.1.call-done), channel_id=1, source_target_pairs={{0,504},{4,508},{8,0},{12,4},{16,8},{20,12},{24,16},{28,20},{32,24... | collective-permute-start | bytes 3538952 | tf_op jit(solution)/shard_map/ppermute | solution.py:12
  52.0 2.9 collective-permute-start.3
  54.9 0.1 fusion.54
  55.1 2.4 collective-permute-start.2
  58.8 2.1 collective-permute-start.1
  60.9 2.2 collective-permute-start
  63.0 39.0 %collective-permute-done.4 = bf16[768,768]{1,0:T(8,128)(2,1)S(1)} collective-permute-done((bf16[768,768]{1,0:T(8,128)(2,1)}, bf16[768,768]{1,0:T(8,128)(2,1)S(1)}, u32[]{:S(2)}, u32[]{:S(2)}) %collective-permute-start.4) | collective-permute-done | bytes 1179680 | tf_op jit(solution)/shard_map/ppermute | solution.py:12
  102.0 0.6 fusion.40
  102.6 0.4 copy-done.3
  103.0 0.6 convolution_convert_fusion
  103.6 2.8 collective-permute-start.9
  106.4 21.5 %collective-permute-done.3 = bf16[768,768]{1,0:T(8,128)(2,1)S(1)} collective-permute-done((bf16[768,768]{1,0:T(8,128)(2,1)}, bf16[768,768]{1,0:T(8,128)(2,1)S(1)}, u32[]{:S(2)}, u32[]{:S(2)}) %collective-permute-start.3) | collective-permute-done | bytes 1179680 | tf_op jit(solution)/shard_map/ppermute | solution.py:12
  127.9 0.6 fusion.41
  128.5 1.6 convolution_convert_fusion.1
  130.1 1.9 collective-permute-start.8
  132.0 0.0 collective-permute-done.2
  132.0 0.6 fusion.43
  132.6 0.4 copy-done.5
  133.1 1.6 convolution_convert_fusion.3
  134.7 8.2 %collective-permute-start.7 = (bf16[768,768]{1,0:T(8,128)(2,1)}, bf16[768,768]{1,0:T(8,128)(2,1)}, u32[]{:S(2)}, u32[]{:S(2)}) collective-permute-start(bf16[768,768]{1,0:T(8,128)(2,1)} %convolution_convert_fusion.3), channel_id=1, source_target_pairs={{0,508},{4,0},{8,4},{12,8},{16,12},{20,16},{24,20},{28,24},{32,28}... | collective-permute-start | bytes 3538952 | tf_op jit(solution)/shard_map/ppermute | solution.py:12
  142.9 0.0 collective-permute-done.1
  142.9 0.6 fusion.44
  143.6 0.4 copy-done.7
  143.9 1.6 convolution_convert_fusion.4
  145.5 34.0 %collective-permute-start.6 = (bf16[768,768]{1,0:T(8,128)(2,1)}, bf16[768,768]{1,0:T(8,128)(2,1)}, u32[]{:S(2)}, u32[]{:S(2)}) collective-permute-start(bf16[768,768]{1,0:T(8,128)(2,1)} %convolution_convert_fusion.4), channel_id=1, source_target_pairs={{0,504},{4,508},{8,0},{12,4},{16,8},{20,12},{24,16},{28,20},{32,24... | collective-permute-start | bytes 3538952 | tf_op jit(solution)/shard_map/ppermute | solution.py:12
  179.5 25.9 %collective-permute-done = bf16[768,768]{1,0:T(8,128)(2,1)S(1)} collective-permute-done((bf16[768,768]{1,0:T(8,128)(2,1)}, bf16[768,768]{1,0:T(8,128)(2,1)S(1)}, u32[]{:S(2)}, u32[]{:S(2)}) %collective-permute-start) | collective-permute-done | bytes 1179680 | tf_op jit(solution)/shard_map/ppermute | solution.py:12
  205.5 0.6 fusion.45
  206.1 0.4 copy-done.9
  206.5 1.6 convolution_convert_fusion.5
  208.1 55.2 %collective-permute-start.5 = (bf16[768,768]{1,0:T(8,128)(2,1)}, bf16[768,768]{1,0:T(8,128)(2,1)}, u32[]{:S(2)}, u32[]{:S(2)}) collective-permute-start(bf16[768,768]{1,0:T(8,128)(2,1)} %convolution_convert_fusion.5), channel_id=1, source_target_pairs={{0,500},{4,504},{8,508},{12,0},{16,4},{20,8},{24,12},{28,16},{32,2... | collective-permute-start | bytes 3538952 | tf_op jit(solution)/shard_map/ppermute | solution.py:12
  263.4 1.9 fusion.42
  265.3 0.0 collective-permute-done.9
  265.3 25.1 %collective-permute-done.8 = bf16[768,768]{1,0:T(8,128)(2,1)} collective-permute-done((bf16[768,768]{1,0:T(8,128)(2,1)}, bf16[768,768]{1,0:T(8,128)(2,1)}, u32[]{:S(2)}, u32[]{:S(2)}) %collective-permute-start.8) | collective-permute-done | bytes 1179680 | tf_op jit(solution)/shard_map/ppermute | solution.py:12
  290.3 0.0 collective-permute-done.7
  290.3 0.0 collective-permute-done.6
  290.3 23.9 %collective-permute-done.5 = bf16[768,768]{1,0:T(8,128)(2,1)} collective-permute-done((bf16[768,768]{1,0:T(8,128)(2,1)}, bf16[768,768]{1,0:T(8,128)(2,1)}, u32[]{:S(2)}, u32[]{:S(2)}) %collective-permute-start.5) | collective-permute-done | bytes 1179680 | tf_op jit(solution)/shard_map/ppermute | solution.py:12
  314.2 4.7 %add_convert_fusion = bf16[768,768]{1,0:T(8,128)(2,1)} fusion(bf16[768,768]{1,0:T(8,128)(2,1)} %collective-permute-done.9, bf16[768,768]{1,0:T(8,128)(2,1)} %collective-permute-done.8, bf16[768,768]{1,0:T(8,128)(2,1)} %collective-permute-done.7, bf16[768,768]{1,0:T(8,128)(2,1)} %collective-permute-done.6, bf16[768,768]{1,0:T(8,128)(2,1)} %collective-permute-done.5, ...), kind=kOutput, calls=%fused_computation | convolution fusion | flops 234602496 | bytes 7668480 | tf_op jit(solution)/shard_map/dot_general | solution.py:67
  318.9 0.0 reduce-scatter.2.cloned.1.call-update
  319.0 1.2 copy-done.2
  320.2 0.4 fusion.72
  320.6 0.9 copy-done.4
  321.5 0.4 fusion.73
  321.9 0.9 copy-done.6
  322.8 0.0 copy-done.12
  322.8 0.4 fusion.71
  323.2 0.9 copy-done.8
  324.1 0.0 copy-done.14
  324.1 0.4 fusion.70
  324.5 0.9 copy-done.10
  325.4 0.0 copy-done.16
  325.4 0.4 fusion.7
  325.9 0.5 fusion.51
  326.4 0.0 copy-start.1
  326.4 1.0 fusion.53
  327.4 99.5 %reduce-scatter.2.cloned.1.call-done = bf16[192,768]{1,0:T(8,128)(2,1)} async-done(((bf16[768,768]{1,0:T(8,128)(2,1)}), bf16[192,768]{1,0:T(8,128)(2,1)}) %reduce-scatter.2.cloned.1.call-update) | async-done | bytes 294928 | tf_op jit(solution)/shard_map/reduce_scatter | solution.py:74
  426.9 1.2 fusion.56
  428.1 2.0 fusion.57
  (23 shorter events, 0.1 us)
Async XLA Ops:
  7.2 47.8 %copy-start = (bf16[192,768]{1,0:T(8,128)(2,1)S(1)}, bf16[192,768]{1,0:T(8,128)(2,1)}, u32[]{:S(2)}) copy-start(bf16[192,768]{1,0:T(8,128)(2,1)} %param.4) | copy-start | bytes 884740
  7.2 36.3 %all-gather.2.cloned.1.call-start = ((), (), s32[]{:S(2)}) async-start(), calls=%async_computation.1 | async-start | bytes 1474560 | tf_op jit(solution)/shard_map/all_gather | solution.py:41
  10.2 416.8 %reduce-scatter.2.cloned.1.call-start = ((), (), s32[]{:S(2)}) async-start(), calls=%async_computation.2 | async-start | bytes 1474560 | tf_op jit(solution)/shard_map/reduce_scatter | solution.py:74
  43.4 58.6 %collective-permute-start.4 = (bf16[768,768]{1,0:T(8,128)(2,1)}, bf16[768,768]{1,0:T(8,128)(2,1)S(1)}, u32[]{:S(2)}, u32[]{:S(2)}) collective-permute-start(bf16[768,768]{1,0:T(8,128)(2,1)} %all-gather.2.cloned.1.call-done), channel_id=1, source_target_pairs={{0,504},{4,508},{8,0},{12,4},{16,8},{20,12},{24,16},{28,20},{32,24... | collective-permute-start | bytes 3538952 | tf_op jit(solution)/shard_map/ppermute | solution.py:12
  52.0 75.9 %collective-permute-start.3 = (bf16[768,768]{1,0:T(8,128)(2,1)}, bf16[768,768]{1,0:T(8,128)(2,1)S(1)}, u32[]{:S(2)}, u32[]{:S(2)}) collective-permute-start(bf16[768,768]{1,0:T(8,128)(2,1)} %all-gather.2.cloned.1.call-done), channel_id=1, source_target_pairs={{0,508},{4,0},{8,4},{12,8},{16,12},{20,16},{24,20},{28,24},{32,28}... | collective-permute-start | bytes 3538952 | tf_op jit(solution)/shard_map/ppermute | solution.py:12
  55.1 76.9 %collective-permute-start.2 = (bf16[768,768]{1,0:T(8,128)(2,1)}, bf16[768,768]{1,0:T(8,128)(2,1)S(1)}, u32[]{:S(2)}, u32[]{:S(2)}) collective-permute-start(bf16[768,768]{1,0:T(8,128)(2,1)} %all-gather.2.cloned.1.call-done), channel_id=1, source_target_pairs={{0,4},{4,8},{8,12},{12,16},{16,20},{20,24},{24,28},{28,32},{32,36}... | collective-permute-start | bytes 3538952 | tf_op jit(solution)/shard_map/ppermute | solution.py:12
  58.8 84.1 %collective-permute-start.1 = (bf16[768,768]{1,0:T(8,128)(2,1)}, bf16[768,768]{1,0:T(8,128)(2,1)S(1)}, u32[]{:S(2)}, u32[]{:S(2)}) collective-permute-start(bf16[768,768]{1,0:T(8,128)(2,1)} %all-gather.2.cloned.1.call-done), channel_id=1, source_target_pairs={{0,8},{4,12},{8,16},{12,20},{16,24},{20,28},{24,32},{28,36},{32,40... | collective-permute-start | bytes 3538952 | tf_op jit(solution)/shard_map/ppermute | solution.py:12
  60.9 144.6 %collective-permute-start = (bf16[768,768]{1,0:T(8,128)(2,1)}, bf16[768,768]{1,0:T(8,128)(2,1)S(1)}, u32[]{:S(2)}, u32[]{:S(2)}) collective-permute-start(bf16[768,768]{1,0:T(8,128)(2,1)} %all-gather.2.cloned.1.call-done), channel_id=1, source_target_pairs={{0,12},{4,16},{8,20},{12,24},{16,28},{20,32},{24,36},{28,40},{32,4... | collective-permute-start | bytes 3538952 | tf_op jit(solution)/shard_map/ppermute | solution.py:12
  102.0 1.0 copy-start.3
  103.6 161.7 %collective-permute-start.9 = (bf16[768,768]{1,0:T(8,128)(2,1)S(1)}, bf16[768,768]{1,0:T(8,128)(2,1)}, u32[]{:S(2)}, u32[]{:S(2)}) collective-permute-start(bf16[768,768]{1,0:T(8,128)(2,1)S(1)} %convolution_convert_fusion), channel_id=1, source_target_pairs={{0,8},{4,12},{8,16},{12,20},{16,24},{20,28},{24,32},{28,36},{32,40... | collective-permute-start | bytes 3538952 | tf_op jit(solution)/shard_map/ppermute | solution.py:12
  130.1 160.2 %collective-permute-start.8 = (bf16[768,768]{1,0:T(8,128)(2,1)}, bf16[768,768]{1,0:T(8,128)(2,1)}, u32[]{:S(2)}, u32[]{:S(2)}) collective-permute-start(bf16[768,768]{1,0:T(8,128)(2,1)} %convolution_convert_fusion.1), channel_id=1, source_target_pairs={{0,4},{4,8},{8,12},{12,16},{16,20},{20,24},{24,28},{28,32},{32,36}... | collective-permute-start | bytes 3538952 | tf_op jit(solution)/shard_map/ppermute | solution.py:12
  132.0 1.0 copy-start.5
  133.1 10.5 %copy-start.11 = (bf16[192,768]{1,0:T(8,128)(2,1)}, bf16[192,768]{1,0:T(8,128)(2,1)S(1)}, u32[]{:S(2)}) copy-start(bf16[192,768]{1,0:T(8,128)(2,1)S(1)} %fusion.43) | copy-start | bytes 884740
  134.7 155.6 %collective-permute-start.7 = (bf16[768,768]{1,0:T(8,128)(2,1)}, bf16[768,768]{1,0:T(8,128)(2,1)}, u32[]{:S(2)}, u32[]{:S(2)}) collective-permute-start(bf16[768,768]{1,0:T(8,128)(2,1)} %convolution_convert_fusion.3), channel_id=1, source_target_pairs={{0,508},{4,0},{8,4},{12,8},{16,12},{20,16},{24,20},{28,24},{32,28}... | collective-permute-start | bytes 3538952 | tf_op jit(solution)/shard_map/ppermute | solution.py:12
  142.9 1.0 copy-start.7
  143.9 62.2 %copy-start.13 = (bf16[192,768]{1,0:T(8,128)(2,1)}, bf16[192,768]{1,0:T(8,128)(2,1)S(1)}, u32[]{:S(2)}) copy-start(bf16[192,768]{1,0:T(8,128)(2,1)S(1)} %fusion.44) | copy-start | bytes 884740
  145.5 144.8 %collective-permute-start.6 = (bf16[768,768]{1,0:T(8,128)(2,1)}, bf16[768,768]{1,0:T(8,128)(2,1)}, u32[]{:S(2)}, u32[]{:S(2)}) collective-permute-start(bf16[768,768]{1,0:T(8,128)(2,1)} %convolution_convert_fusion.4), channel_id=1, source_target_pairs={{0,504},{4,508},{8,0},{12,4},{16,8},{20,12},{24,16},{28,20},{32,24... | collective-permute-start | bytes 3538952 | tf_op jit(solution)/shard_map/ppermute | solution.py:12
  205.5 1.0 copy-start.9
  206.5 56.8 %copy-start.15 = (bf16[192,768]{1,0:T(8,128)(2,1)}, bf16[192,768]{1,0:T(8,128)(2,1)S(1)}, u32[]{:S(2)}) copy-start(bf16[192,768]{1,0:T(8,128)(2,1)S(1)} %fusion.45) | copy-start | bytes 884740
  208.1 106.1 %collective-permute-start.5 = (bf16[768,768]{1,0:T(8,128)(2,1)}, bf16[768,768]{1,0:T(8,128)(2,1)}, u32[]{:S(2)}, u32[]{:S(2)}) collective-permute-start(bf16[768,768]{1,0:T(8,128)(2,1)} %convolution_convert_fusion.5), channel_id=1, source_target_pairs={{0,500},{4,504},{8,508},{12,0},{16,4},{20,8},{24,12},{28,16},{32,2... | collective-permute-start | bytes 3538952 | tf_op jit(solution)/shard_map/ppermute | solution.py:12
  318.9 1.3 copy-start.2
  320.2 1.3 copy-start.4
  321.5 1.3 copy-start.6
  321.5 1.3 copy-start.12
  322.8 1.3 copy-start.8
  322.8 1.3 copy-start.14
  324.1 1.3 copy-start.10
  324.1 1.3 copy-start.16
  326.4 100.6 %copy-start.1 = (bf16[192,768]{1,0:T(8,128)(2,1)S(1)}, bf16[192,768]{1,0:T(8,128)(2,1)}, u32[]{:S(2)}) copy-start(bf16[192,768]{1,0:T(8,128)(2,1)} %param.5) | copy-start | bytes 884740
Sparse Core Ops, SparseCore 0:
  10.7 32.7 all-gather.1
  319.1 107.7 reduce-scatter.1
where the time goes:
time: 438 us; the launch traced here: 437 us
  waiting for transfers between devices  268 us (61%)
  starting transfers between devices  120 us (27%)
  matrix products  19.1 us (4%)
  between operations  15.6 us (4%)
  other arithmetic  7.33 us (2%)
  local copies, waits for them, and re-layouts  6.47 us (1%)
    ppermute x10, waiting for transfers between devices, passed_along(): return lax.ppermute(value, axis, pairs)  135 us
    ppermute x10, starting transfers between devices, passed_along(): return lax.ppermute(value, axis, pairs)  120 us
    reduce_scatter x1, waiting for transfers between devices, local(): lax.psum_scatter(returned.astype(jnp.bfloat16), 'grp', scatter_dimension=...  99.5 us
    all_gather x1, waiting for transfers between devices, local(): source = lax.all_gather(yb, 'grp', axis=0, tiled=True)  33.2 us
    dot_general x6, matrix products, local(): lax.dot_general(coef, xb, (((0,), (0,)), ((), ())), preferred_element_typ...  11.7 us
  transfers between devices with their start and end apart: 12, of which 7 were waited for; matrix products, arithmetic and copies ran while one was open for 4% of the time, Pallas kernels for 0%

commit v1 on v0

v1 whole, which is shorter than its diff:
```python
import functools

import jax
import jax.numpy as jnp
from jax import lax
from jax.experimental import pallas as pl
from jax.experimental.pallas import tpu as pltpu
from jax.sharding import PartitionSpec as P

MESH = pl.DeviceIdType.MESH
R = 192
D = 768
RUN = 8
N = 4
C = R // N
F32 = jnp.float32
BF16 = jnp.bfloat16

OWN, M1, M2, M3, P1, P2 = 0, 1, 2, 3, 4, 5


def inv_norm(wide):
    return lax.rsqrt(jnp.sum(wide * wide, axis=-1, keepdims=True) + 1e-06)


def back_rows(values, grad):
    wide = values.astype(F32)
    scale = inv_norm(wide)
    unit = wide * scale
    return scale * (grad - unit * jnp.sum(unit * grad, axis=-1, keepdims=True))


def kernel(
    nb, x_ref, y_ref, s_ref, b_ref, gx_ref, gy_ref,
    xf, ys, ct, part, accs, accr, gsend, grecv, xsend, xrecv, gown,
    ysend, yrecv, asend, arecv, gs, gr,
):
    b = lax.axis_index("blk")
    g = lax.axis_index("grp")
    core = lax.rem(g, 2)
    spot = lax.rem(b, 2 * RUN)
    last = jnp.where(core == 0, 2 * RUN - 1, RUN - 1)
    first = jnp.where(core == 0, 0, RUN)
    partner = lax.rem(g + 2, 4)
    nxt = (lax.rem(b + 1, nb), jnp.where(spot == last, partner, g))
    prv = (lax.rem(b + nb - 1, nb), jnp.where(spot == first, partner, g))
    xp = (b, partner)
    cp = (b, g + 1 - 2 * core)

    barrier = pltpu.get_barrier_semaphore()
    for who in (nxt, prv, xp, cp):
        pl.semaphore_signal(barrier, inc=1, device_id=who, device_id_type=MESH)

    def rows(slot, c):
        return pl.ds(pl.multiple_of(slot * R + c * C, 16), C)

    def copy(src, dst, ssem, rsem, who):
        return pltpu.make_async_remote_copy(
            src_ref=src, dst_ref=dst, send_sem=ssem, recv_sem=rsem, device_id=who, device_id_type=MESH
        )

    kinds = ((OWN, M1, nxt), (M1, M2, nxt), (M2, M3, nxt), (OWN, P1, prv), (P1, P2, prv))

    def piece(kind, c):
        src, dst, who = kinds[kind]
        return copy(ys.at[rows(src, c)], ys.at[rows(dst, c)], ysend.at[kind, c], yrecv.at[kind, c], who)

    def acc(kind, c):
        who = prv if kind < 3 else nxt
        return copy(accs.at[rows(kind, c)], accr.at[rows(kind, c)], asend.at[kind, c], arecv.at[kind, c], who)

    def block(k, count=1):
        return pl.ds(k * R, count * R)

    gather_x = copy(xf.at[block(0)], xf.at[block(1)], gs.at[0], gr.at[0], xp)
    gather_c = copy(xf.at[block(0)], xf.at[block(2)], gs.at[1], gr.at[1], cp)
    gather_d = copy(xf.at[block(1)], xf.at[block(3)], gs.at[2], gr.at[2], cp)
    reduce_c = copy(gsend, grecv, gs.at[3], gr.at[3], cp)
    reduce_x = copy(xsend, xrecv, gs.at[4], gr.at[4], xp)

    def loop(body):
        lax.fori_loop(0, N, lambda c, _: (body(c), 0)[1], 0)

    wide = y_ref[...].astype(F32)
    ys[block(OWN)] = (wide * inv_norm(wide)).astype(BF16)
    pl.semaphore_wait(barrier, 4)

    @loop
    def _(c):
        piece(0, c).start()
        piece(3, c).start()

    wide = x_ref[...].astype(F32)
    xf[block(0)] = (wide * inv_norm(wide)).astype(BF16)
    gather_x.start()
    gather_c.start()

    @loop
    def _(c):
        piece(0, c).wait_recv()
        piece(1, c).start()
        piece(3, c).wait_recv()
        piece(4, c).start()

    gather_x.wait_recv()
    gather_d.start()
    gather_c.wait_recv()
    gather_d.wait_recv()

    scale = s_ref[0]
    bias = b_ref[0]

    def task(slot, c):
        y = ys[rows(slot, c)]
        dots = lax.dot_general(y, xf[...], (((1,), (1,)), ((), ())), preferred_element_type=F32)
        z = scale * dots + bias
        if slot == OWN:
            here = lax.broadcasted_iota(jnp.int32, (C, 4 * R), 1) == (
                lax.broadcasted_iota(jnp.int32, (C, 4 * R), 0) + c * C
            )
            sign = jnp.where(here, -1.0, 1.0).astype(F32)
            coef = sign * scale / (1.0 + jnp.exp(-sign * z))
        else:
            coef = scale / (1.0 + jnp.exp(-z))
        coef = coef.astype(BF16)
        ct[rows(slot, c)] = coef
        return jnp.dot(coef, xf[...], preferred_element_type=F32)

    @loop
    def _(c):
        piece(1, c).wait_recv()
        piece(2, c).start()
        part[rows(0, c)] = task(OWN, c)
        part[rows(1, c)] = task(M1, c)
        piece(4, c).wait_recv()
        accs[rows(3, c)] = task(P2, c).astype(BF16)

    @loop
    def _(c):
        piece(2, c).wait_recv()
        accs[rows(0, c)] = task(M3, c).astype(BF16)
        acc(0, c).start()
        acc(3, c).start()
        part[rows(2, c)] = task(M2, c)
        part[rows(3, c)] = task(P1, c)

    def pass_on(src, mine, dst, c):
        acc(src, c).wait_recv()
        accs[rows(dst, c)] = (part[rows(mine, c)] + accr[rows(src, c)].astype(F32)).astype(BF16)
        acc(dst, c).start()

    @loop
    def _(c):
        pass_on(0, 2, 1, c)
        pass_on(3, 3, 4, c)

    def grads(lo):
        return lax.dot_general(
            ct[:, lo * R : (lo + 2) * R], ys[...], (((0,), (0,)), ((), ())), preferred_element_type=F32
        )

    gsend[...] = grads(2).astype(BF16)
    reduce_c.start()
    gown[...] = grads(0)
    reduce_c.wait_recv()
    xsend[...] = (gown[block(1)] + grecv[block(1)].astype(F32)).astype(BF16)
    reduce_x.start()

    @loop
    def _(c):
        pass_on(1, 1, 2, c)

    @loop
    def _(c):
        acc(4, c).wait_recv()
        acc(2, c).wait_recv()
        grad = part[rows(0, c)] + accr[rows(4, c)].astype(F32) + accr[rows(2, c)].astype(F32)
        gy_ref[rows(0, c)] = back_rows(y_ref[rows(0, c)], grad)

    reduce_x.wait_recv()
    total = gown[block(0)] + grecv[block(0)].astype(F32) + xrecv[...].astype(F32)
    gx_ref[...] = back_rows(x_ref[...], total)

    @loop
    def _(c):
        for kind in range(5):
            piece(kind, c).wait_send()
            acc(kind, c).wait_send()

    for one in (gather_x, gather_c, gather_d, reduce_c, reduce_x):
        one.wait_send()


def solution(mesh):
    nb = mesh.shape["blk"]

    def local(x, y, s, b):
        vmem = pl.BlockSpec(memory_space=pltpu.VMEM)
        smem = pl.BlockSpec(memory_space=pltpu.SMEM)
        dma = pltpu.SemaphoreType.DMA
        return pl.pallas_call(
            functools.partial(kernel, nb),
            out_shape=[jax.ShapeDtypeStruct((R, D), F32)] * 2,
            in_specs=[vmem, vmem, smem, smem],
            out_specs=[vmem, vmem],
            scratch_shapes=[
                pltpu.VMEM((4 * R, D), BF16),
                pltpu.VMEM((6 * R, D), BF16),
                pltpu.VMEM((6 * R, 4 * R), BF16),
                pltpu.VMEM((4 * R, D), F32),
                pltpu.VMEM((5 * R, D), BF16),
                pltpu.VMEM((5 * R, D), BF16),
                pltpu.VMEM((2 * R, D), BF16),
                pltpu.VMEM((2 * R, D), BF16),
                pltpu.VMEM((R, D), BF16),
                pltpu.VMEM((R, D), BF16),
                pltpu.VMEM((2 * R, D), F32),
                dma((5, N)),
                dma((5, N)),
                dma((5, N)),
                dma((5, N)),
                dma((5,)),
                dma((5,)),
            ],
            compiler_params=pltpu.CompilerParams(
                collective_id=0, has_side_effects=True, vmem_limit_bytes=48 * 2**20
            ),
            cost_estimate=pl.CostEstimate(flops=4 * 10**9, bytes_accessed=2 * 10**6, transcendentals=10**6),
        )(x, y, s, b)

    spec = P(("blk", "grp"), None)
    return jax.shard_map(
        local, mesh=mesh, in_specs=(spec, spec, P(), P()), out_specs=(spec, spec), check_vma=False
    )
```

time: 438 us -> 69.7 us (0.16)
  waiting for transfers between devices: 268 us -> 0 us
  starting transfers between devices: 120 us -> 0 us
  Pallas kernels: 0 us -> 64 us
  matrix products: 19.1 us -> 0 us
  between operations: 15.6 us -> 1.94 us
  other arithmetic: 7.33 us -> 0 us
    ppermute x10 -> x0, waiting for transfers between devices: 135 us -> none  [passed_along(): return lax.ppermute(value, axis, pairs)]
    ppermute x10 -> x0, starting transfers between devices: 120 us -> none  [passed_along(): return lax.ppermute(value, axis, pairs)]
    reduce_scatter x1 -> x0, waiting for transfers between devices: 99.5 us -> none  [local(): lax.psum_scatter(returned.astype(jnp.bfloat16), 'grp', scatter_dimension=...]
    pallas_call x0 -> x1, Pallas kernels: none -> 64 us  [local(): pl.pallas_call(functools.partial(kernel, nb), out_shape=[jax.ShapeDtypeSt...]
    all_gather x1 -> x0, waiting for transfers between devices: 33.2 us -> none  [local(): source = lax.all_gather(yb, 'grp', axis=0, tiled=True)]
    dot_general x18 -> x0, matrix products: 19.1 us -> none  [the longest x6 11.7 us: local(): lax.dot_general(coef, xb, (((0,), (0,)), ((), ())), preferred_element_typ...]
  transfers between devices with their start and end apart: 12 -> 0, of which waited for: 7 -> 0; matrix products, arithmetic and copies ran while one was open for 4% -> 0% of each run, Pallas kernels for 0% -> 0%
where the time goes in v1:
time: 69.7 us; the launch traced here: 69.5 us
  Pallas kernels  64 us (92%)
  local copies, waits for them, and re-layouts  3.55 us (5%)
  between operations  1.94 us (3%)
    pallas_call x1, Pallas kernels, local(): pl.pallas_call(functools.partial(kernel, nb), out_shape=[jax.ShapeDtypeSt...  64 us
    unnamed x6, local copies, waits for them, and re-layouts  3.55 us

profile of v1, /device:TPU:1, one launch (start us, length us, event | category | flops | bytes accessed | tf_op | source)
XLA Modules:
  0.0 69.5 jit_solution(1451998760852028111)
XLA Ops:
  1.9 0.0 copy-start
  1.9 1.0 %copy-done = bf16[192,768]{1,0:T(8,128)(2,1)S(1)} copy-done((bf16[192,768]{1,0:T(8,128)(2,1)S(1)}, bf16[192,768]{1,0:T(8,128)(2,1)}, u32[]{:S(2)}) %copy-start) | copy-done | bytes 294936
  2.9 0.0 copy-start.1
  2.9 1.0 %copy-done.1 = bf16[192,768]{1,0:T(8,128)(2,1)S(1)} copy-done((bf16[192,768]{1,0:T(8,128)(2,1)S(1)}, bf16[192,768]{1,0:T(8,128)(2,1)}, u32[]{:S(2)}) %copy-start.1) | copy-done | bytes 294936
  3.8 64.0 %shard_map.59 = (f32[192,768]{1,0:T(8,128)S(1)}, f32[192,768]{1,0:T(8,128)S(1)}) custom-call(bf16[192,768]{1,0:T(8,128)(2,1)S(1)} %copy-done, bf16[192,768]{1,0:T(8,128)(2,1)S(1)} %copy-done.1, f32[1]{0:T(128)S(6)} %copy.8.s_ref, f32[1]{0:T(128)S(6)} %copy.9.b_ref), custom_call_target="tpu_custom_call" | custom-call | flops 4000000000 | bytes 2000000 | tf_op jit(solution)/shard_map/pallas_call | solution.py:201
  67.9 0.8 %copy.10 = f32[192,768]{1,0:T(8,128)} copy(f32[192,768]{1,0:T(8,128)S(1)} %get-tuple-element.4) | data formatting | bytes 1179648
  68.7 0.8 %copy.11 = f32[192,768]{1,0:T(8,128)} copy(f32[192,768]{1,0:T(8,128)S(1)} %get-tuple-element.5) | data formatting | bytes 1179648
Async XLA Ops:
  1.9 1.0 %copy-start = (bf16[192,768]{1,0:T(8,128)(2,1)S(1)}, bf16[192,768]{1,0:T(8,128)(2,1)}, u32[]{:S(2)}) copy-start(bf16[192,768]{1,0:T(8,128)(2,1)} %x_ref.1) | copy-start | bytes 884740
  2.9 1.0 %copy-start.1 = (bf16[192,768]{1,0:T(8,128)(2,1)S(1)}, bf16[192,768]{1,0:T(8,128)(2,1)}, u32[]{:S(2)}) copy-start(bf16[192,768]{1,0:T(8,128)(2,1)} %y_ref.1) | copy-start | bytes 884740

commit v2 on v1

--- a/solution.py
+++ b/solution.py
@@ -12,11 +12,12 @@
 D = 768
 RUN = 8
 N = 4
+G = 1
 C = R // N
 F32 = jnp.float32
 BF16 = jnp.bfloat16
 
-OWN, M1, M2, M3, P1, P2 = 0, 1, 2, 3, 4, 5
+OWN, M1, P1, P2, M2, M3 = 0, 1, 2, 3, 4, 5
 
 
 def inv_norm(wide):
@@ -31,9 +32,9 @@
 
 
 def kernel(
-    nb, x_ref, y_ref, s_ref, b_ref, gx_ref, gy_ref,
-    xf, ys, ct, part, accs, accr, gsend, grecv, xsend, xrecv, gown,
-    ysend, yrecv, asend, arecv, gs, gr,
+    nb, x_hbm, y_hbm, s_ref, b_ref, gx_ref, gy_ref,
+    x_ref, y_ref, xf, ys, ct, part, accs, accr, gsend, grecv, xsend, xrecv, gown,
+    ysend, yrecv, asend, arecv, gs, gr, ls,
 ):
     b = lax.axis_index("blk")
     g = lax.axis_index("grp")
@@ -51,6 +52,11 @@
     for who in (nxt, prv, xp, cp):
         pl.semaphore_signal(barrier, inc=1, device_id=who, device_id_type=MESH)
 
+    load_y = pltpu.make_async_copy(y_hbm, y_ref, ls.at[0])
+    load_x = pltpu.make_async_copy(x_hbm, x_ref, ls.at[1])
+    load_y.start()
+    load_x.start()
+
     def rows(slot, c):
         return pl.ds(pl.multiple_of(slot * R + c * C, 16), C)
 
@@ -81,8 +87,12 @@
     def loop(body):
         lax.fori_loop(0, N, lambda c, _: (body(c), 0)[1], 0)
 
+    load_y.wait()
     wide = y_ref[...].astype(F32)
     ys[block(OWN)] = (wide * inv_norm(wide)).astype(BF16)
+    load_x.wait()
+    wide = x_ref[...].astype(F32)
+    xf[block(0)] = (wide * inv_norm(wide)).astype(BF16)
     pl.semaphore_wait(barrier, 4)
 
     @loop
@@ -90,8 +100,6 @@
         piece(0, c).start()
         piece(3, c).start()
 
-    wide = x_ref[...].astype(F32)
-    xf[block(0)] = (wide * inv_norm(wide)).astype(BF16)
     gather_x.start()
     gather_c.start()
 
@@ -101,7 +109,6 @@
         piece(1, c).start()
         piece(3, c).wait_recv()
         piece(4, c).start()
-
     gather_x.wait_recv()
     gather_d.start()
     gather_c.wait_recv()
@@ -110,39 +117,75 @@
     scale = s_ref[0]
     bias = b_ref[0]
 
-    def task(slot, c):
-        y = ys[rows(slot, c)]
+    keep = {OWN: 0, M1: 1, M2: 2, P1: 3}
+    send = {M3: 0, P2: 3}
+
+    def task(slot, c, count):
+        size = count * C
+        spot = pl.ds(pl.multiple_of(slot * R + c * C, 16), size)
+        y = ys[spot]
         dots = lax.dot_general(y, xf[...], (((1,), (1,)), ((), ())), preferred_element_type=F32)
         z = scale * dots + bias
         if slot == OWN:
-            here = lax.broadcasted_iota(jnp.int32, (C, 4 * R), 1) == (
-                lax.broadcasted_iota(jnp.int32, (C, 4 * R), 0) + c * C
+            here = lax.broadcasted_iota(jnp.int32, (size, 4 * R), 1) == (
+                lax.broadcasted_iota(jnp.int32, (size, 4 * R), 0) + c * C
             )
             sign = jnp.where(here, -1.0, 1.0).astype(F32)
             coef = sign * scale / (1.0 + jnp.exp(-sign * z))
         else:
             coef = scale / (1.0 + jnp.exp(-z))
         coef = coef.astype(BF16)
-        ct[rows(slot, c)] = coef
-        return jnp.dot(coef, xf[...], preferred_element_type=F32)
-
-    @loop
-    def _(c):
+        ct[spot] = coef
+        grad = jnp.dot(coef, xf[...], preferred_element_type=F32)
+        if slot in keep:
+            part[pl.ds(pl.multiple_of(keep[slot] * R + c * C, 16), size)] = grad
+        else:
+            accs[pl.ds(pl.multiple_of(send[slot] * R + c * C, 16), size)] = grad.astype(BF16)
+
+    def forward(c):
         piece(1, c).wait_recv()
         piece(2, c).start()
-        part[rows(0, c)] = task(OWN, c)
-        part[rows(1, c)] = task(M1, c)
+
+    for c in range(N):
+        forward(c)
+        if c < 3:
+            task((OWN, M1, P1)[c], 0, N)
+    for slot in (OWN, M1, P1)[N:]:
+        task(slot, 0, N)
+
+    @loop
+    def _(c):
         piece(4, c).wait_recv()
-        accs[rows(3, c)] = task(P2, c).astype(BF16)
-
-    @loop
-    def _(c):
-        piece(2, c).wait_recv()
-        accs[rows(0, c)] = task(M3, c).astype(BF16)
-        acc(0, c).start()
-        acc(3, c).start()
-        part[rows(2, c)] = task(M2, c)
-        part[rows(3, c)] = task(P1, c)
+
+    task(P2, 0, N)
+    task(M2, 0, N)
+
+    def grads(lo, first, last):
+        k = pl.ds(first * R, (last - first) * R)
+        return lax.dot_general(
+            ct[k, lo * R : (lo + 2) * R], ys[k], (((0,), (0,)), ((), ())), preferred_element_type=F32
+        )
+
+    gown[block(0, 2)] = grads(0, OWN, M3)
+    gown[block(2, 2)] = grads(2, OWN, M3)
+
+    def last_piece(q, _):
+        for k in range(G):
+            piece(2, q * G + k).wait_recv()
+        task(M3, q * G, G)
+        for k in range(G):
+            acc(0, q * G + k).start()
+            acc(3, q * G + k).start()
+        return 0
+
+    lax.fori_loop(0, N // G, last_piece, 0)
+
+    gsend[...] = (gown[block(2, 2)] + grads(2, M3, M3 + 1)).astype(BF16)
+    reduce_c.start()
+    gown[block(0, 2)] += grads(0, M3, M3 + 1)
+    reduce_c.wait_recv()
+    xsend[...] = (gown[block(1)] + grecv[block(1)].astype(F32)).astype(BF16)
+    reduce_x.start()
 
     def pass_on(src, mine, dst, c):
         acc(src, c).wait_recv()
@@ -154,18 +197,6 @@
         pass_on(0, 2, 1, c)
         pass_on(3, 3, 4, c)
 
-    def grads(lo):
-        return lax.dot_general(
-            ct[:, lo * R : (lo + 2) * R], ys[...], (((0,), (0,)), ((), ())), preferred_element_type=F32
-        )
-
-    gsend[...] = grads(2).astype(BF16)
-    reduce_c.start()
-    gown[...] = grads(0)
-    reduce_c.wait_recv()
-    xsend[...] = (gown[block(1)] + grecv[block(1)].astype(F32)).astype(BF16)
-    reduce_x.start()
-
     @loop
     def _(c):
         pass_on(1, 1, 2, c)
@@ -195,15 +226,18 @@
     nb = mesh.shape["blk"]
 
     def local(x, y, s, b):
+        hbm = pl.BlockSpec(memory_space=pl.ANY)
         vmem = pl.BlockSpec(memory_space=pltpu.VMEM)
         smem = pl.BlockSpec(memory_space=pltpu.SMEM)
         dma = pltpu.SemaphoreType.DMA
         return pl.pallas_call(
             functools.partial(kernel, nb),
             out_shape=[jax.ShapeDtypeStruct((R, D), F32)] * 2,
-            in_specs=[vmem, vmem, smem, smem],
+            in_specs=[hbm, hbm, smem, smem],
             out_specs=[vmem, vmem],
             scratch_shapes=[
+                pltpu.VMEM((R, D), BF16),
+                pltpu.VMEM((R, D), BF16),
                 pltpu.VMEM((4 * R, D), BF16),
                 pltpu.VMEM((6 * R, D), BF16),
                 pltpu.VMEM((6 * R, 4 * R), BF16),
@@ -214,13 +248,14 @@
                 pltpu.VMEM((2 * R, D), BF16),
                 pltpu.VMEM((R, D), BF16),
                 pltpu.VMEM((R, D), BF16),
-                pltpu.VMEM((2 * R, D), F32),
+                pltpu.VMEM((4 * R, D), F32),
                 dma((5, N)),
                 dma((5, N)),
                 dma((5, N)),
                 dma((5, N)),
                 dma((5,)),
                 dma((5,)),
+                dma((2,)),
             ],
             compiler_params=pltpu.CompilerParams(
                 collective_id=0, has_side_effects=True, vmem_limit_bytes=48 * 2**20

time: 69.7 us -> 63.4 us (0.910)
  Pallas kernels: 64 us -> 57.7 us
    pallas_call x1, Pallas kernels: 64 us -> 57.7 us  [local(): pl.pallas_call(functools.partial(kernel, nb), out_shape=[jax.ShapeDtypeSt...]
where the time goes in v2:
time: 63.4 us; the launch traced here: 63.2 us
  Pallas kernels  57.7 us (91%)
  local copies, waits for them, and re-layouts  3.55 us (6%)
  between operations  1.94 us (3%)
    pallas_call x1, Pallas kernels, local(): pl.pallas_call(functools.partial(kernel, nb), out_shape=[jax.ShapeDtypeSt...  57.7 us
    unnamed x6, local copies, waits for them, and re-layouts  3.55 us

profile of v2, /device:TPU:1, one launch (start us, length us, event | category | flops | bytes accessed | tf_op | source)
XLA Modules:
  0.0 63.2 jit_solution(833568932025614730)
XLA Ops:
  1.9 0.0 copy-start
  1.9 1.0 %copy-done = bf16[192,768]{1,0:T(8,128)(2,1)S(1)} copy-done((bf16[192,768]{1,0:T(8,128)(2,1)S(1)}, bf16[192,768]{1,0:T(8,128)(2,1)}, u32[]{:S(2)}) %copy-start) | copy-done | bytes 294936
  2.9 0.0 copy-start.1
  2.9 1.0 %copy-done.1 = bf16[192,768]{1,0:T(8,128)(2,1)S(1)} copy-done((bf16[192,768]{1,0:T(8,128)(2,1)S(1)}, bf16[192,768]{1,0:T(8,128)(2,1)}, u32[]{:S(2)}) %copy-start.1) | copy-done | bytes 294936
  3.8 57.7 %shard_map.59 = (f32[192,768]{1,0:T(8,128)S(1)}, f32[192,768]{1,0:T(8,128)S(1)}) custom-call(bf16[192,768]{1,0:T(8,128)(2,1)S(1)} %copy-done, bf16[192,768]{1,0:T(8,128)(2,1)S(1)} %copy-done.1, f32[1]{0:T(128)S(6)} %copy.8.s_ref, f32[1]{0:T(128)S(6)} %copy.9.b_ref), custom_call_target="tpu_custom_call" | custom-call | flops 4000000000 | bytes 2000000 | tf_op jit(solution)/shard_map/pallas_call | solution.py:233
  61.5 0.8 %copy.10 = f32[192,768]{1,0:T(8,128)} copy(f32[192,768]{1,0:T(8,128)S(1)} %get-tuple-element.4) | data formatting | bytes 1179648
  62.4 0.8 %copy.11 = f32[192,768]{1,0:T(8,128)} copy(f32[192,768]{1,0:T(8,128)S(1)} %get-tuple-element.5) | data formatting | bytes 1179648
Async XLA Ops:
  1.9 1.0 %copy-start = (bf16[192,768]{1,0:T(8,128)(2,1)S(1)}, bf16[192,768]{1,0:T(8,128)(2,1)}, u32[]{:S(2)}) copy-start(bf16[192,768]{1,0:T(8,128)(2,1)} %x_hbm.1) | copy-start | bytes 884740
  2.9 1.0 %copy-start.1 = (bf16[192,768]{1,0:T(8,128)(2,1)S(1)}, bf16[192,768]{1,0:T(8,128)(2,1)}, u32[]{:S(2)}) copy-start(bf16[192,768]{1,0:T(8,128)(2,1)} %y_hbm.1) | copy-start | bytes 884740

commit v3 on v2

--- a/solution.py
+++ b/solution.py
@@ -32,10 +32,11 @@
 
 
 def kernel(
-    nb, x_hbm, y_hbm, s_ref, b_ref, gx_ref, gy_ref,
-    x_ref, y_ref, xf, ys, ct, part, accs, accr, gsend, grecv, xsend, xrecv, gown,
-    ysend, yrecv, asend, arecv, gs, gr, ls,
+    nb, xy_ref, s_ref, b_ref, gx_ref, gy_ref,
+    xf, xt, ys, ct, part, accs, accr, gsend, grecv, xsend, xrecv, gown,
+    ysend, yrecv, asend, arecv, gs, gr,
 ):
+    x_ref, y_ref = xy_ref.at[pl.ds(0, R)], xy_ref.at[pl.ds(R, R)]
     b = lax.axis_index("blk")
     g = lax.axis_index("grp")
     core = lax.rem(g, 2)
@@ -52,11 +53,6 @@
     for who in (nxt, prv, xp, cp):
         pl.semaphore_signal(barrier, inc=1, device_id=who, device_id_type=MESH)
 
-    load_y = pltpu.make_async_copy(y_hbm, y_ref, ls.at[0])
-    load_x = pltpu.make_async_copy(x_hbm, x_ref, ls.at[1])
-    load_y.start()
-    load_x.start()
-
     def rows(slot, c):
         return pl.ds(pl.multiple_of(slot * R + c * C, 16), C)
 
@@ -87,10 +83,8 @@
     def loop(body):
         lax.fori_loop(0, N, lambda c, _: (body(c), 0)[1], 0)
 
-    load_y.wait()
     wide = y_ref[...].astype(F32)
     ys[block(OWN)] = (wide * inv_norm(wide)).astype(BF16)
-    load_x.wait()
     wide = x_ref[...].astype(F32)
     xf[block(0)] = (wide * inv_norm(wide)).astype(BF16)
     pl.semaphore_wait(barrier, 4)
@@ -113,6 +107,7 @@
     gather_d.start()
     gather_c.wait_recv()
     gather_d.wait_recv()
+    xt[...] = xf[...].T
 
     scale = s_ref[0]
     bias = b_ref[0]
@@ -124,7 +119,7 @@
         size = count * C
         spot = pl.ds(pl.multiple_of(slot * R + c * C, 16), size)
         y = ys[spot]
-        dots = lax.dot_general(y, xf[...], (((1,), (1,)), ((), ())), preferred_element_type=F32)
+        dots = jnp.dot(y, xt[...], preferred_element_type=F32)
         z = scale * dots + bias
         if slot == OWN:
             here = lax.broadcasted_iota(jnp.int32, (size, 4 * R), 1) == (
@@ -222,6 +217,17 @@
         one.wait_send()
 
 
+def store(gx_ref, gy_ref, gx_hbm, gy_hbm, sems):
+    copies = [
+        pltpu.make_async_copy(gx_ref, gx_hbm, sems.at[0]),
+        pltpu.make_async_copy(gy_ref, gy_hbm, sems.at[1]),
+    ]
+    for one in copies:
+        one.start()
+    for one in copies:
+        one.wait()
+
+
 def solution(mesh):
     nb = mesh.shape["blk"]
 
@@ -230,14 +236,14 @@
         vmem = pl.BlockSpec(memory_space=pltpu.VMEM)
         smem = pl.BlockSpec(memory_space=pltpu.SMEM)
         dma = pltpu.SemaphoreType.DMA
-        return pl.pallas_call(
+        rows = jnp.concatenate([x, y])
+        grads = pl.pallas_call(
             functools.partial(kernel, nb),
             out_shape=[jax.ShapeDtypeStruct((R, D), F32)] * 2,
-            in_specs=[hbm, hbm, smem, smem],
+            in_specs=[vmem, smem, smem],
             out_specs=[vmem, vmem],
             scratch_shapes=[
-                pltpu.VMEM((R, D), BF16),
-                pltpu.VMEM((R, D), BF16),
+                pltpu.VMEM((4 * R, D), BF16),
                 pltpu.VMEM((4 * R, D), BF16),
                 pltpu.VMEM((6 * R, D), BF16),
                 pltpu.VMEM((6 * R, 4 * R), BF16),
@@ -255,13 +261,20 @@
                 dma((5, N)),
                 dma((5,)),
                 dma((5,)),
-                dma((2,)),
             ],
             compiler_params=pltpu.CompilerParams(
                 collective_id=0, has_side_effects=True, vmem_limit_bytes=48 * 2**20
             ),
             cost_estimate=pl.CostEstimate(flops=4 * 10**9, bytes_accessed=2 * 10**6, transcendentals=10**6),
-        )(x, y, s, b)
+        )(rows, s, b)
+        return pl.pallas_call(
+            store,
+            out_shape=[jax.ShapeDtypeStruct((R, D), F32)] * 2,
+            in_specs=[vmem, vmem],
+            out_specs=[hbm, hbm],
+            scratch_shapes=[dma((2,))],
+            compiler_params=pltpu.CompilerParams(vmem_limit_bytes=4 * 2**20),
+        )(*grads)
 
     spec = P(("blk", "grp"), None)
     return jax.shard_map(

time: 63.4 us -> 61.6 us (0.972)
  local copies, waits for them, and re-layouts: 3.55 us -> 0 us
  other arithmetic: 0 us -> 1.09 us
  Pallas kernels: 57.7 us -> 58.4 us
    unnamed x6 -> x0, local copies, waits for them, and re-layouts: 3.55 us -> none
    concatenate x0 -> x1, other arithmetic: none -> 1.09 us  [local(): rows = jnp.concatenate([x, y])]
    pallas_call x0 -> x1, Pallas kernels: none -> 1.03 us  [local(): pl.pallas_call(store, out_shape=[jax.ShapeDtypeStruct((R, D), F32)] * 2,...]
where the time goes in v3:
time: 61.6 us; the launch traced here: 61.5 us
  Pallas kernels  58.4 us (95%)
  between operations  1.93 us (3%)
  other arithmetic  1.09 us (2%)
    pallas_call x1, Pallas kernels, local(): pl.pallas_call(functools.partial(kernel, nb), out_shape=[jax.ShapeDtypeSt...  57.4 us

profile of v3, /device:TPU:1, one launch (start us, length us, event | category | flops | bytes accessed | tf_op | source)
XLA Modules:
  0.0 61.5 jit_solution(6550736024171834824)
XLA Ops:
  1.9 1.1 %pad_maximum_fusion.xy_ref = bf16[384,768]{1,0:T(8,128)(2,1)S(1)} fusion(bf16[192,768]{1,0:T(8,128)(2,1)} %param.5, bf16[192,768]{1,0:T(8,128)(2,1)} %param.4), kind=kLoop, calls=%fused_computation | loop fusion | flops 1179648 | bytes 1179648 | tf_op jit(solution)/shard_map/concatenate | solution.py:239
  3.0 57.4 %shard_map.59 = (f32[192,768]{1,0:T(8,128)S(1)}, f32[192,768]{1,0:T(8,128)S(1)}) custom-call(bf16[384,768]{1,0:T(8,128)(2,1)S(1)} %pad_maximum_fusion.xy_ref, f32[1]{0:T(128)S(6)} %copy.6.s_ref, f32[1]{0:T(128)S(6)} %copy.7.b_ref), custom_call_target="tpu_custom_call" | custom-call | flops 4000000000 | bytes 2000000 | tf_op jit(solution)/shard_map/pallas_call | solution.py:240
  60.4 1.0 %shard_map.60 = (f32[192,768]{1,0:T(8,128)}, f32[192,768]{1,0:T(8,128)}) custom-call(f32[192,768]{1,0:T(8,128)S(1)} %get-tuple-element.4.gx_ref, f32[192,768]{1,0:T(8,128)S(1)} %get-tuple-element.5.gy_ref), custom_call_target="tpu_custom_call" | custom-call | tf_op jit(solution)/shard_map/pallas_call | solution.py:270

commit v4 on v3

--- a/solution.py
+++ b/solution.py
@@ -50,7 +50,7 @@
     cp = (b, g + 1 - 2 * core)
 
     barrier = pltpu.get_barrier_semaphore()
-    for who in (nxt, prv, xp, cp):
+    for who in (xp, nxt, prv, cp):
         pl.semaphore_signal(barrier, inc=1, device_id=who, device_id_type=MESH)
 
     def rows(slot, c):
@@ -196,16 +196,16 @@
     def _(c):
         pass_on(1, 1, 2, c)
 
+    reduce_x.wait_recv()
+    total = gown[block(0)] + grecv[block(0)].astype(F32) + xrecv[...].astype(F32)
+    gx_ref[...] = back_rows(x_ref[...], total)
+
     @loop
     def _(c):
         acc(4, c).wait_recv()
         acc(2, c).wait_recv()
         grad = part[rows(0, c)] + accr[rows(4, c)].astype(F32) + accr[rows(2, c)].astype(F32)
         gy_ref[rows(0, c)] = back_rows(y_ref[rows(0, c)], grad)
-
-    reduce_x.wait_recv()
-    total = gown[block(0)] + grecv[block(0)].astype(F32) + xrecv[...].astype(F32)
-    gx_ref[...] = back_rows(x_ref[...], total)
 
     @loop
     def _(c):

time: 61.6 us -> 61.3 us (level)
  no operation moved by 1% of the time
where the time goes in v4:
time: 61.3 us; the launch traced here: 61.2 us
  Pallas kernels  58.1 us (95%)
  between operations  1.93 us (3%)
  other arithmetic  1.09 us (2%)
    pallas_call x1, Pallas kernels, local(): pl.pallas_call(functools.partial(kernel, nb), out_shape=[jax.ShapeDtypeSt...  57.1 us

profile of v4, /device:TPU:1, one launch (start us, length us, event | category | flops | bytes accessed | tf_op | source)
XLA Modules:
  0.0 61.2 jit_solution(953251705232995824)
XLA Ops:
  1.9 1.1 %pad_maximum_fusion.xy_ref = bf16[384,768]{1,0:T(8,128)(2,1)S(1)} fusion(bf16[192,768]{1,0:T(8,128)(2,1)} %param.5, bf16[192,768]{1,0:T(8,128)(2,1)} %param.4), kind=kLoop, calls=%fused_computation | loop fusion | flops 1179648 | bytes 1179648 | tf_op jit(solution)/shard_map/concatenate | solution.py:239
  3.0 57.1 %shard_map.59 = (f32[192,768]{1,0:T(8,128)S(1)}, f32[192,768]{1,0:T(8,128)S(1)}) custom-call(bf16[384,768]{1,0:T(8,128)(2,1)S(1)} %pad_maximum_fusion.xy_ref, f32[1]{0:T(128)S(6)} %copy.6.s_ref, f32[1]{0:T(128)S(6)} %copy.7.b_ref), custom_call_target="tpu_custom_call" | custom-call | flops 4000000000 | bytes 2000000 | tf_op jit(solution)/shard_map/pallas_call | solution.py:240
  60.1 1.0 %shard_map.60 = (f32[192,768]{1,0:T(8,128)}, f32[192,768]{1,0:T(8,128)}) custom-call(f32[192,768]{1,0:T(8,128)S(1)} %get-tuple-element.4.gx_ref, f32[192,768]{1,0:T(8,128)S(1)} %get-tuple-element.5.gy_ref), custom_call_target="tpu_custom_call" | custom-call | tf_op jit(solution)/shard_map/pallas_call | solution.py:270

commit v5 on v4

--- a/solution.py
+++ b/solution.py
@@ -103,8 +103,14 @@
         piece(1, c).start()
         piece(3, c).wait_recv()
         piece(4, c).start()
+
+    def forward(c):
+        piece(1, c).wait_recv()
+        piece(2, c).start()
+
     gather_x.wait_recv()
     gather_d.start()
+    forward(0)
     gather_c.wait_recv()
     gather_d.wait_recv()
     xt[...] = xf[...].T
@@ -137,12 +143,9 @@
         else:
             accs[pl.ds(pl.multiple_of(send[slot] * R + c * C, 16), size)] = grad.astype(BF16)
 
-    def forward(c):
-        piece(1, c).wait_recv()
-        piece(2, c).start()
-
     for c in range(N):
-        forward(c)
+        if c > 0:
+            forward(c)
         if c < 3:
             task((OWN, M1, P1)[c], 0, N)
     for slot in (OWN, M1, P1)[N:]:

time: 61.3 us -> 61 us (level)
  no operation moved by 1% of the time
where the time goes in v5:
time: 61 us; the launch traced here: 60.8 us
  Pallas kernels  57.8 us (95%)
  between operations  1.93 us (3%)
  other arithmetic  1.09 us (2%)
    pallas_call x1, Pallas kernels, local(): pl.pallas_call(functools.partial(kernel, nb), out_shape=[jax.ShapeDtypeSt...  56.8 us

profile of v5, /device:TPU:1, one launch (start us, length us, event | category | flops | bytes accessed | tf_op | source)
XLA Modules:
  0.0 60.8 jit_solution(2183277398384699698)
XLA Ops:
  1.9 1.1 %pad_maximum_fusion.xy_ref = bf16[384,768]{1,0:T(8,128)(2,1)S(1)} fusion(bf16[192,768]{1,0:T(8,128)(2,1)} %param.5, bf16[192,768]{1,0:T(8,128)(2,1)} %param.4), kind=kLoop, calls=%fused_computation | loop fusion | flops 1179648 | bytes 1179648 | tf_op jit(solution)/shard_map/concatenate | solution.py:242
  3.0 56.8 %shard_map.59 = (f32[192,768]{1,0:T(8,128)S(1)}, f32[192,768]{1,0:T(8,128)S(1)}) custom-call(bf16[384,768]{1,0:T(8,128)(2,1)S(1)} %pad_maximum_fusion.xy_ref, f32[1]{0:T(128)S(6)} %copy.6.s_ref, f32[1]{0:T(128)S(6)} %copy.7.b_ref), custom_call_target="tpu_custom_call" | custom-call | flops 4000000000 | bytes 2000000 | tf_op jit(solution)/shard_map/pallas_call | solution.py:243
  59.8 1.0 %shard_map.60 = (f32[192,768]{1,0:T(8,128)}, f32[192,768]{1,0:T(8,128)}) custom-call(f32[192,768]{1,0:T(8,128)S(1)} %get-tuple-element.4.gx_ref, f32[192,768]{1,0:T(8,128)S(1)} %get-tuple-element.5.gy_ref), custom_call_target="tpu_custom_call" | custom-call | tf_op jit(solution)/shard_map/pallas_call | solution.py:273

commit v6 on v5

--- a/solution.py
+++ b/solution.py
@@ -113,6 +113,7 @@
     forward(0)
     gather_c.wait_recv()
     gather_d.wait_recv()
+    forward(1)
     xt[...] = xf[...].T
 
     scale = s_ref[0]
@@ -144,7 +145,7 @@
             accs[pl.ds(pl.multiple_of(send[slot] * R + c * C, 16), size)] = grad.astype(BF16)
 
     for c in range(N):
-        if c > 0:
+        if c > 1:
             forward(c)
         if c < 3:
             task((OWN, M1, P1)[c], 0, N)

time: 61 us -> 60.8 us (level)
  no operation moved by 1% of the time
where the time goes in v6:
time: 60.8 us; the launch traced here: 60.6 us
  Pallas kernels  57.6 us (95%)
  between operations  1.93 us (3%)
  other arithmetic  1.09 us (2%)
    pallas_call x1, Pallas kernels, local(): pl.pallas_call(functools.partial(kernel, nb), out_shape=[jax.ShapeDtypeSt...  56.6 us

profile of v6, /device:TPU:1, one launch (start us, length us, event | category | flops | bytes accessed | tf_op | source)
XLA Modules:
  0.0 60.6 jit_solution(2030618982778517153)
XLA Ops:
  1.9 1.1 %pad_maximum_fusion.xy_ref = bf16[384,768]{1,0:T(8,128)(2,1)S(1)} fusion(bf16[192,768]{1,0:T(8,128)(2,1)} %param.5, bf16[192,768]{1,0:T(8,128)(2,1)} %param.4), kind=kLoop, calls=%fused_computation | loop fusion | flops 1179648 | bytes 1179648 | tf_op jit(solution)/shard_map/concatenate | solution.py:243
  3.0 56.6 %shard_map.59 = (f32[192,768]{1,0:T(8,128)S(1)}, f32[192,768]{1,0:T(8,128)S(1)}) custom-call(bf16[384,768]{1,0:T(8,128)(2,1)S(1)} %pad_maximum_fusion.xy_ref, f32[1]{0:T(128)S(6)} %copy.6.s_ref, f32[1]{0:T(128)S(6)} %copy.7.b_ref), custom_call_target="tpu_custom_call" | custom-call | flops 4000000000 | bytes 2000000 | tf_op jit(solution)/shard_map/pallas_call | solution.py:244
  59.6 1.0 %shard_map.60 = (f32[192,768]{1,0:T(8,128)}, f32[192,768]{1,0:T(8,128)}) custom-call(f32[192,768]{1,0:T(8,128)S(1)} %get-tuple-element.4.gx_ref, f32[192,768]{1,0:T(8,128)S(1)} %get-tuple-element.5.gy_ref), custom_call_target="tpu_custom_call" | custom-call | tf_op jit(solution)/shard_map/pallas_call | solution.py:274
